TPU v7x, 256 devices: a whole 4x4x8 slice. The times are simulated.
256 devices in a mesh: section: 16 (over y, x), expert: 16 (over z, core).
Axes of the slice: x: 4, y: 4, z: 8, core: 2. Of those that a mesh axis runs over, the one named last changes fastest.
Arguments:
- layer_inputs: bfloat16 [16, 16, 128, 4096], P('section', None, 'expert'), may hold values from -6 to 6
- expert_ids: int32 [16, 16, 128, 2], P('section', None, 'expert'), may hold values from 0 to 7, all different within a row; in each aligned block of 8 rows (0 to 7, 8 to 15, ..., all dimensions but the last counted through in order) at most 3 rows name the same one
- gates: bfloat16 [16, 16, 128, 2], P('section', None, 'expert'), may hold values from 0.099609375 to 0.59765625
- w_gate: bfloat16 [16, 4096, 4096], P('section', None, 'expert'), may hold values from -0.09375 to 0.09375
- w_up: bfloat16 [16, 4096, 4096], P('section', None, 'expert'), may hold values from -0.09375 to 0.09375
- w_down: bfloat16 [16, 4096, 4096], P('section', 'expert'), may hold values from -0.25 to 0.25
- out_grad: bfloat16 [16, 128, 4096], P(None, 'expert'), may hold values from -6 to 6
Outputs:
- section_grads: bfloat16 [16, 16, 128, 4096], P('section', None, 'expert')
Inputs may be any that keep to these rules, and one draw needn't show every extreme that they name: `expert_ids`: within one micro-batch of one section, the 8 tokens of one expert index name each expert at most 3 times, and in some such groups one expert exactly 3 times; a token's 2 experts differ.
All inputs are finite; a program needn't handle non-finite values.
Results may differ from a plain program's by a relative error of at most 0.035.
Values may be sent and summed in bfloat16 or wider, within the bound.
A program may use at most 64 MiB of HBM per device.

v0:
```python
import jax
import jax.numpy as jnp
from jax import lax
from jax.sharding import PartitionSpec as P

EXPERTS = 8
CAP = 3


def passed_along(x, axis, by):
    length = lax.axis_size(axis)
    pairs = [(i, i + by) for i in range(length) if 0 <= i + by < length]
    return lax.ppermute(x, axis, pairs)


def selection(choices, capacity):
    token_count, top_count = (choices.shape[-2], choices.shape[-1])
    experts = jnp.arange(EXPERTS, dtype=jnp.int32)
    onehot = (choices[..., None] == experts).astype(jnp.int32)
    leading = onehot.shape[:-3]
    flattened = onehot.reshape(leading + (token_count * top_count, EXPERTS))
    before = jnp.cumsum(flattened, axis=-2) - flattened
    slot_index = jnp.sum((before * flattened).reshape(onehot.shape), axis=-1)
    places = jnp.arange(capacity, dtype=jnp.int32)
    in_slot = (slot_index[..., None] == places).astype(jnp.int32)
    return onehot[..., None] * in_slot[..., None, :]


def on_device(layer_inputs, expert_ids, gates, w_gate, w_up, w_down, out_grad):
    expert_count = lax.axis_size("expert")
    section_count = lax.axis_size("section")
    section_index = lax.axis_index("section")
    inputs = layer_inputs[0]
    gate_slice = w_gate[0]
    up_slice = w_up[0]
    down_slice = w_down[0]
    micro_count, token_count, model_width = inputs.shape
    hidden = gate_slice.shape[1]
    shards = expert_count // EXPERTS
    capacity = CAP
    slot_rows = expert_count * capacity
    contract = (((1,), (1,)), ((), ()))
    selected = selection(expert_ids[0], capacity)
    dispatch = jnp.sum(selected, axis=2).astype(jnp.bfloat16)
    gate_values = gates[0].astype(jnp.float32)
    combine = jnp.sum(selected.astype(jnp.float32) * gate_values[..., None, None], axis=2).astype(
        jnp.bfloat16
    )

    def spread(rows):
        leading = rows.shape[:-3]
        rows = rows.astype(jnp.bfloat16)
        rows = jnp.broadcast_to(
            jnp.expand_dims(rows, -3), leading + (EXPERTS, shards, capacity, model_width)
        )
        return rows.reshape(leading + (expert_count, capacity, model_width))

    def backward_rows(grad_block, act, coef):
        down_grad = lax.dot_general(
            grad_block, down_slice, contract, preferred_element_type=jnp.float32
        )
        dgate = (down_grad * coef).astype(jnp.bfloat16)
        dup = (down_grad * act).astype(jnp.bfloat16)
        total = lax.dot_general(dgate, gate_slice, contract, preferred_element_type=jnp.float32)
        total = total + lax.dot_general(dup, up_slice, contract, preferred_element_type=jnp.float32)
        return total.astype(jnp.bfloat16)

    zeros_back = jnp.zeros((slot_rows, model_width), jnp.bfloat16)
    outgoing = spread(
        jnp.einsum("mtec,mtd->mecd", dispatch, inputs, preferred_element_type=jnp.float32)
    )
    received = lax.all_to_all(outgoing, "expert", split_axis=1, concat_axis=1, tiled=True)
    item_count = received.shape[0]
    row_block = received.reshape(-1, model_width)
    pre_gate = jnp.dot(row_block, gate_slice, preferred_element_type=jnp.float32)
    pre_up = jnp.dot(row_block, up_slice, preferred_element_type=jnp.float32)
    sigmoid_gate = jax.nn.sigmoid(pre_gate)
    act = pre_gate * sigmoid_gate
    coef = pre_up * (sigmoid_gate * (1.0 + pre_gate * (1.0 - sigmoid_gate)))
    act, coef = (act, coef)
    saved = jnp.stack([act, coef]).reshape(2, item_count, slot_rows, hidden)
    act_all = saved[0]
    coef_all = saved[1]

    def tick(tick_index, state_pair):
        incoming, results = state_pair
        micro_index = tick_index - (section_count - 1 - section_index)
        active = (micro_index >= 0) & (micro_index < micro_count)
        micro_slot = jnp.clip(micro_index, 0, micro_count - 1)
        top_grad = lax.dynamic_index_in_dim(out_grad, micro_slot, 0, keepdims=False)
        grad_out = jnp.where(section_index == section_count - 1, top_grad, incoming)
        dispatch_micro = lax.dynamic_index_in_dim(dispatch, micro_slot, 0, keepdims=False)
        combine_micro = lax.dynamic_index_in_dim(combine, micro_slot, 0, keepdims=False)
        grad_rows = spread(
            jnp.einsum("tec,td->ecd", dispatch_micro, grad_out, preferred_element_type=jnp.float32)
        )
        arrived = lax.all_to_all(
            grad_rows, "expert", split_axis=0, concat_axis=0, tiled=True
        ).reshape(slot_rows, model_width)

        def local_saved(row_block):
            act = lax.dynamic_index_in_dim(act_all, micro_slot, 0, keepdims=False)
            coef = lax.dynamic_index_in_dim(coef_all, micro_slot, 0, keepdims=False)
            return backward_rows(row_block, act, coef)

        def skip_saved(row_block):
            return zeros_back

        back = lax.cond(active, local_saved, skip_saved, arrived)
        returned = lax.all_to_all(
            back.reshape(expert_count, capacity, model_width),
            "expert",
            split_axis=0,
            concat_axis=0,
            tiled=True,
        )
        returned = returned.reshape(EXPERTS, shards, capacity, model_width)
        mixed = jnp.einsum(
            "tec,ekcd->td", combine_micro, returned, preferred_element_type=jnp.float32
        )
        grad_in = (grad_out.astype(jnp.float32) + mixed).astype(jnp.bfloat16)
        updated = lax.dynamic_update_index_in_dim(results, grad_in, micro_slot, 0)
        results = jnp.where(active, updated, results)
        passed = passed_along(grad_in, "section", -1)
        return (passed, results)

    initial = (
        jnp.zeros((token_count, model_width), jnp.bfloat16),
        jnp.zeros((micro_count, token_count, model_width), jnp.bfloat16),
    )
    final_state = lax.fori_loop(0, micro_count + section_count - 1, tick, initial)
    return final_state[1][None]


def solution(mesh):
    placed = (
        P("section", None, "expert", None),
        P("section", None, "expert", None),
        P("section", None, "expert", None),
        P("section", None, "expert"),
        P("section", None, "expert"),
        P("section", "expert", None),
        P(None, "expert", None),
    )
    return jax.shard_map(
        on_device,
        mesh=mesh,
        in_specs=placed,
        out_specs=P("section", None, "expert", None),
        check_vma=False,
    )
```

profile of v0, /device:TPU:32, one launch (start us, length us, event | category | flops | bytes accessed | tf_op | source)
XLA Modules:
  0.0 2027.4 jit_solution(850015349437797174)
XLA Ops:
  18.0 136.6 %all-to-all-done.2 = bf16[16,16,3,4096]{3,0,2,1:T(8,128)(2,1)} async-done(((bf16[16,16,3,4096]{3,0,2,1:T(8,128)(2,1)}), bf16[16,16,3,4096]{3,0,2,1:T(8,128)(2,1)}, u32[]{:S(2)}, u32[]{:S(2)}) %all-to-all-start.2) | async-done | bytes 6291488 | tf_op jit(solution)/shard_map/all_to_all | solution.py:72
  189.4 1838.0 %while.17 = (s32[]{:T(128)}, bf16[8,4096]{1,0:T(8,128)(2,1)S(1)}, bf16[16,8,4096]{2,1,0:T(8,128)(2,1)}, pred[]{:T(512)}, s32[]{:T(128)}, /*index=5*/bf16[16,8,40...) while((s32[]{:T(128)}, bf16[8,4096]{1,0:T(8,128)(2,1)S(1)}, ...), condition=%wide.region_8.9_spmd, body=%wide.region_4.8_spmd.sunk | while | flops 306167808 | bytes 32488984 | solution.py:131
  198.6 14.5 all-to-all-done
  214.1 20.5 %all_to_all.29 = bf16[16,3,4096]{2,1,0:T(4,128)(2,1)S(1)} all-to-all(bf16[16,3,4096]{2,1,0:T(4,128)(2,1)} %reshape.87), channel_id=1, replica_groups=mesh['section'=16,'expert'=16] {'expert'}, dimensions={0} | all-to-all | bytes 786432 | tf_op jit(solution)/shard_map/while/body/eval_jaxpr/all_to_all | solution.py:110
  251.2 14.4 all-to-all-done
  266.7 20.6 %all_to_all.29 = bf16[16,3,4096]{2,1,0:T(4,128)(2,1)S(1)} all-to-all(bf16[16,3,4096]{2,1,0:T(4,128)(2,1)} %reshape.87), channel_id=1, replica_groups=mesh['section'=16,'expert'=16] {'expert'}, dimensions={0} | all-to-all | bytes 786432 | tf_op jit(solution)/shard_map/while/body/eval_jaxpr/all_to_all | solution.py:110
  303.8 14.4 all-to-all-done
  319.3 20.6 %all_to_all.29 = bf16[16,3,4096]{2,1,0:T(4,128)(2,1)S(1)} all-to-all(bf16[16,3,4096]{2,1,0:T(4,128)(2,1)} %reshape.87), channel_id=1, replica_groups=mesh['section'=16,'expert'=16] {'expert'}, dimensions={0} | all-to-all | bytes 786432 | tf_op jit(solution)/shard_map/while/body/eval_jaxpr/all_to_all | solution.py:110
  372.0 20.6 %all_to_all.29 = bf16[16,3,4096]{2,1,0:T(4,128)(2,1)S(1)} all-to-all(bf16[16,3,4096]{2,1,0:T(4,128)(2,1)} %reshape.87), channel_id=1, replica_groups=mesh['section'=16,'expert'=16] {'expert'}, dimensions={0} | all-to-all | bytes 786432 | tf_op jit(solution)/shard_map/while/body/eval_jaxpr/all_to_all | solution.py:110
  409.0 14.4 all-to-all-done
  424.5 20.6 %all_to_all.29 = bf16[16,3,4096]{2,1,0:T(4,128)(2,1)S(1)} all-to-all(bf16[16,3,4096]{2,1,0:T(4,128)(2,1)} %reshape.87), channel_id=1, replica_groups=mesh['section'=16,'expert'=16] {'expert'}, dimensions={0} | all-to-all | bytes 786432 | tf_op jit(solution)/shard_map/while/body/eval_jaxpr/all_to_all | solution.py:110
  463.6 14.5 all-to-all-done
  479.2 20.5 %all_to_all.29 = bf16[16,3,4096]{2,1,0:T(4,128)(2,1)S(1)} all-to-all(bf16[16,3,4096]{2,1,0:T(4,128)(2,1)} %reshape.87), channel_id=1, replica_groups=mesh['section'=16,'expert'=16] {'expert'}, dimensions={0} | all-to-all | bytes 786432 | tf_op jit(solution)/shard_map/while/body/eval_jaxpr/all_to_all | solution.py:110
  518.3 14.5 all-to-all-done
  534.0 20.5 %all_to_all.29 = bf16[16,3,4096]{2,1,0:T(4,128)(2,1)S(1)} all-to-all(bf16[16,3,4096]{2,1,0:T(4,128)(2,1)} %reshape.87), channel_id=1, replica_groups=mesh['section'=16,'expert'=16] {'expert'}, dimensions={0} | all-to-all | bytes 786432 | tf_op jit(solution)/shard_map/while/body/eval_jaxpr/all_to_all | solution.py:110
  573.1 14.5 all-to-all-done
  588.7 20.5 %all_to_all.29 = bf16[16,3,4096]{2,1,0:T(4,128)(2,1)S(1)} all-to-all(bf16[16,3,4096]{2,1,0:T(4,128)(2,1)} %reshape.87), channel_id=1, replica_groups=mesh['section'=16,'expert'=16] {'expert'}, dimensions={0} | all-to-all | bytes 786432 | tf_op jit(solution)/shard_map/while/body/eval_jaxpr/all_to_all | solution.py:110
  627.9 14.5 all-to-all-done
  643.5 20.5 %all_to_all.29 = bf16[16,3,4096]{2,1,0:T(4,128)(2,1)S(1)} all-to-all(bf16[16,3,4096]{2,1,0:T(4,128)(2,1)} %reshape.87), channel_id=1, replica_groups=mesh['section'=16,'expert'=16] {'expert'}, dimensions={0} | all-to-all | bytes 786432 | tf_op jit(solution)/shard_map/while/body/eval_jaxpr/all_to_all | solution.py:110
  682.6 14.5 all-to-all-done
  698.2 20.5 %all_to_all.29 = bf16[16,3,4096]{2,1,0:T(4,128)(2,1)S(1)} all-to-all(bf16[16,3,4096]{2,1,0:T(4,128)(2,1)} %reshape.87), channel_id=1, replica_groups=mesh['section'=16,'expert'=16] {'expert'}, dimensions={0} | all-to-all | bytes 786432 | tf_op jit(solution)/shard_map/while/body/eval_jaxpr/all_to_all | solution.py:110
  737.4 14.5 all-to-all-done
  753.0 20.5 %all_to_all.29 = bf16[16,3,4096]{2,1,0:T(4,128)(2,1)S(1)} all-to-all(bf16[16,3,4096]{2,1,0:T(4,128)(2,1)} %reshape.87), channel_id=1, replica_groups=mesh['section'=16,'expert'=16] {'expert'}, dimensions={0} | all-to-all | bytes 786432 | tf_op jit(solution)/shard_map/while/body/eval_jaxpr/all_to_all | solution.py:110
  792.1 14.5 all-to-all-done
  807.8 20.5 %all_to_all.29 = bf16[16,3,4096]{2,1,0:T(4,128)(2,1)S(1)} all-to-all(bf16[16,3,4096]{2,1,0:T(4,128)(2,1)} %reshape.87), channel_id=1, replica_groups=mesh['section'=16,'expert'=16] {'expert'}, dimensions={0} | all-to-all | bytes 786432 | tf_op jit(solution)/shard_map/while/body/eval_jaxpr/all_to_all | solution.py:110
  846.9 14.5 all-to-all-done
  862.5 20.5 %all_to_all.29 = bf16[16,3,4096]{2,1,0:T(4,128)(2,1)S(1)} all-to-all(bf16[16,3,4096]{2,1,0:T(4,128)(2,1)} %reshape.87), channel_id=1, replica_groups=mesh['section'=16,'expert'=16] {'expert'}, dimensions={0} | all-to-all | bytes 786432 | tf_op jit(solution)/shard_map/while/body/eval_jaxpr/all_to_all | solution.py:110
  901.7 14.5 all-to-all-done
  917.3 20.5 %all_to_all.29 = bf16[16,3,4096]{2,1,0:T(4,128)(2,1)S(1)} all-to-all(bf16[16,3,4096]{2,1,0:T(4,128)(2,1)} %reshape.87), channel_id=1, replica_groups=mesh['section'=16,'expert'=16] {'expert'}, dimensions={0} | all-to-all | bytes 786432 | tf_op jit(solution)/shard_map/while/body/eval_jaxpr/all_to_all | solution.py:110
  956.4 14.5 all-to-all-done
  972.0 20.5 %all_to_all.29 = bf16[16,3,4096]{2,1,0:T(4,128)(2,1)S(1)} all-to-all(bf16[16,3,4096]{2,1,0:T(4,128)(2,1)} %reshape.87), channel_id=1, replica_groups=mesh['section'=16,'expert'=16] {'expert'}, dimensions={0} | all-to-all | bytes 786432 | tf_op jit(solution)/shard_map/while/body/eval_jaxpr/all_to_all | solution.py:110
  996.0 61.6 %collective-permute-done = bf16[8,4096]{1,0:T(8,128)(2,1)S(1)} collective-permute-done((bf16[8,4096]{1,0:T(8,128)(2,1)S(1)}, bf16[8,4096]{1,0:T(8,128)(2,1)S(1)}, u32[]{:S(2)}, u32[]{:S(2)}) %collective-permute-start) | collective-permute-done | bytes 65568 | tf_op jit(solution)/shard_map/while/body/eval_jaxpr/ppermute | solution.py:13
  1065.5 14.5 all-to-all-done
  1087.1 20.5 %all_to_all.29 = bf16[16,3,4096]{2,1,0:T(4,128)(2,1)S(1)} all-to-all(bf16[16,3,4096]{2,1,0:T(4,128)(2,1)} %reshape.87), channel_id=1, replica_groups=mesh['section'=16,'expert'=16] {'expert'}, dimensions={0} | all-to-all | bytes 786432 | tf_op jit(solution)/shard_map/while/body/eval_jaxpr/all_to_all | solution.py:110
  1126.3 14.5 all-to-all-done
  1147.9 20.5 %all_to_all.29 = bf16[16,3,4096]{2,1,0:T(4,128)(2,1)S(1)} all-to-all(bf16[16,3,4096]{2,1,0:T(4,128)(2,1)} %reshape.87), channel_id=1, replica_groups=mesh['section'=16,'expert'=16] {'expert'}, dimensions={0} | all-to-all | bytes 786432 | tf_op jit(solution)/shard_map/while/body/eval_jaxpr/all_to_all | solution.py:110
  1187.0 14.5 all-to-all-done
  1208.6 20.5 %all_to_all.29 = bf16[16,3,4096]{2,1,0:T(4,128)(2,1)S(1)} all-to-all(bf16[16,3,4096]{2,1,0:T(4,128)(2,1)} %reshape.87), channel_id=1, replica_groups=mesh['section'=16,'expert'=16] {'expert'}, dimensions={0} | all-to-all | bytes 786432 | tf_op jit(solution)/shard_map/while/body/eval_jaxpr/all_to_all | solution.py:110
  1247.8 14.5 all-to-all-done
  1269.4 20.5 %all_to_all.29 = bf16[16,3,4096]{2,1,0:T(4,128)(2,1)S(1)} all-to-all(bf16[16,3,4096]{2,1,0:T(4,128)(2,1)} %reshape.87), channel_id=1, replica_groups=mesh['section'=16,'expert'=16] {'expert'}, dimensions={0} | all-to-all | bytes 786432 | tf_op jit(solution)/shard_map/while/body/eval_jaxpr/all_to_all | solution.py:110
  1308.6 14.5 all-to-all-done
  1330.2 20.5 %all_to_all.29 = bf16[16,3,4096]{2,1,0:T(4,128)(2,1)S(1)} all-to-all(bf16[16,3,4096]{2,1,0:T(4,128)(2,1)} %reshape.87), channel_id=1, replica_groups=mesh['section'=16,'expert'=16] {'expert'}, dimensions={0} | all-to-all | bytes 786432 | tf_op jit(solution)/shard_map/while/body/eval_jaxpr/all_to_all | solution.py:110
  1369.3 14.5 all-to-all-done
  1390.9 20.5 %all_to_all.29 = bf16[16,3,4096]{2,1,0:T(4,128)(2,1)S(1)} all-to-all(bf16[16,3,4096]{2,1,0:T(4,128)(2,1)} %reshape.87), channel_id=1, replica_groups=mesh['section'=16,'expert'=16] {'expert'}, dimensions={0} | all-to-all | bytes 786432 | tf_op jit(solution)/shard_map/while/body/eval_jaxpr/all_to_all | solution.py:110
  1430.1 14.5 all-to-all-done
  1451.7 20.5 %all_to_all.29 = bf16[16,3,4096]{2,1,0:T(4,128)(2,1)S(1)} all-to-all(bf16[16,3,4096]{2,1,0:T(4,128)(2,1)} %reshape.87), channel_id=1, replica_groups=mesh['section'=16,'expert'=16] {'expert'}, dimensions={0} | all-to-all | bytes 786432 | tf_op jit(solution)/shard_map/while/body/eval_jaxpr/all_to_all | solution.py:110
  1490.9 14.5 all-to-all-done
  1512.5 20.5 %all_to_all.29 = bf16[16,3,4096]{2,1,0:T(4,128)(2,1)S(1)} all-to-all(bf16[16,3,4096]{2,1,0:T(4,128)(2,1)} %reshape.87), channel_id=1, replica_groups=mesh['section'=16,'expert'=16] {'expert'}, dimensions={0} | all-to-all | bytes 786432 | tf_op jit(solution)/shard_map/while/body/eval_jaxpr/all_to_all | solution.py:110
  1551.6 14.5 all-to-all-done
  1573.2 20.5 %all_to_all.29 = bf16[16,3,4096]{2,1,0:T(4,128)(2,1)S(1)} all-to-all(bf16[16,3,4096]{2,1,0:T(4,128)(2,1)} %reshape.87), channel_id=1, replica_groups=mesh['section'=16,'expert'=16] {'expert'}, dimensions={0} | all-to-all | bytes 786432 | tf_op jit(solution)/shard_map/while/body/eval_jaxpr/all_to_all | solution.py:110
  1612.4 14.5 all-to-all-done
  1634.0 20.5 %all_to_all.29 = bf16[16,3,4096]{2,1,0:T(4,128)(2,1)S(1)} all-to-all(bf16[16,3,4096]{2,1,0:T(4,128)(2,1)} %reshape.87), channel_id=1, replica_groups=mesh['section'=16,'expert'=16] {'expert'}, dimensions={0} | all-to-all | bytes 786432 | tf_op jit(solution)/shard_map/while/body/eval_jaxpr/all_to_all | solution.py:110
  1673.1 14.5 all-to-all-done
  1694.7 20.5 %all_to_all.29 = bf16[16,3,4096]{2,1,0:T(4,128)(2,1)S(1)} all-to-all(bf16[16,3,4096]{2,1,0:T(4,128)(2,1)} %reshape.87), channel_id=1, replica_groups=mesh['section'=16,'expert'=16] {'expert'}, dimensions={0} | all-to-all | bytes 786432 | tf_op jit(solution)/shard_map/while/body/eval_jaxpr/all_to_all | solution.py:110
  1733.9 14.5 all-to-all-done
  1755.5 20.5 %all_to_all.29 = bf16[16,3,4096]{2,1,0:T(4,128)(2,1)S(1)} all-to-all(bf16[16,3,4096]{2,1,0:T(4,128)(2,1)} %reshape.87), channel_id=1, replica_groups=mesh['section'=16,'expert'=16] {'expert'}, dimensions={0} | all-to-all | bytes 786432 | tf_op jit(solution)/shard_map/while/body/eval_jaxpr/all_to_all | solution.py:110
  1794.7 14.5 all-to-all-done
  1816.3 20.5 %all_to_all.29 = bf16[16,3,4096]{2,1,0:T(4,128)(2,1)S(1)} all-to-all(bf16[16,3,4096]{2,1,0:T(4,128)(2,1)} %reshape.87), channel_id=1, replica_groups=mesh['section'=16,'expert'=16] {'expert'}, dimensions={0} | all-to-all | bytes 786432 | tf_op jit(solution)/shard_map/while/body/eval_jaxpr/all_to_all | solution.py:110
  1855.4 14.5 all-to-all-done
  1877.0 20.5 %all_to_all.29 = bf16[16,3,4096]{2,1,0:T(4,128)(2,1)S(1)} all-to-all(bf16[16,3,4096]{2,1,0:T(4,128)(2,1)} %reshape.87), channel_id=1, replica_groups=mesh['section'=16,'expert'=16] {'expert'}, dimensions={0} | all-to-all | bytes 786432 | tf_op jit(solution)/shard_map/while/body/eval_jaxpr/all_to_all | solution.py:110
  1916.2 14.5 all-to-all-done
  1937.9 20.5 %all_to_all.29 = bf16[16,3,4096]{2,1,0:T(4,128)(2,1)S(1)} all-to-all(bf16[16,3,4096]{2,1,0:T(4,128)(2,1)} %reshape.87), channel_id=1, replica_groups=mesh['section'=16,'expert'=16] {'expert'}, dimensions={0} | all-to-all | bytes 786432 | tf_op jit(solution)/shard_map/while/body/eval_jaxpr/all_to_all | solution.py:110
  1977.0 14.5 all-to-all-done
  1998.6 20.5 %all_to_all.29 = bf16[16,3,4096]{2,1,0:T(4,128)(2,1)S(1)} all-to-all(bf16[16,3,4096]{2,1,0:T(4,128)(2,1)} %reshape.87), channel_id=1, replica_groups=mesh['section'=16,'expert'=16] {'expert'}, dimensions={0} | all-to-all | bytes 786432 | tf_op jit(solution)/shard_map/while/body/eval_jaxpr/all_to_all | solution.py:110
  (670 shorter events, 852.7 us)
Async XLA Ops:
  8.5 146.1 %all-to-all-start.2 = ((bf16[16,16,3,4096]{3,0,2,1:T(8,128)(2,1)}), bf16[16,16,3,4096]{3,0,2,1:T(8,128)(2,1)}, u32[]{:S(2)}, u32[]{:S(2)}) async-start(bf16[16,16,3,4096]{3,0,2,1:T(8,128)(2,1)} %bitcast.92), calls=%async_computation.2 | async-start | bytes 12582912 | tf_op jit(solution)/shard_map/all_to_all | solution.py:72
  192.0 21.1 %all-to-all-start = ((bf16[16,3,4096]{2,1,0:T(4,128)(2,1)}), bf16[16,3,4096]{2,1,0:T(4,128)(2,1)}, u32[]{:S(2)}, u32[]{:S(2)}) async-start(bf16[16,3,4096]{2,1,0:T(4,128)(2,1)} %bitcast.91), calls=%async_computation | async-start | bytes 1048576 | tf_op jit(solution)/shard_map/while/body/eval_jaxpr/all_to_all | solution.py:97
  236.8 6.1 collective-permute-start
  245.2 20.4 %all-to-all-start = ((bf16[16,3,4096]{2,1,0:T(4,128)(2,1)}), bf16[16,3,4096]{2,1,0:T(4,128)(2,1)}, u32[]{:S(2)}, u32[]{:S(2)}) async-start(bf16[16,3,4096]{2,1,0:T(4,128)(2,1)} %bitcast.91), calls=%async_computation | async-start | bytes 1048576 | tf_op jit(solution)/shard_map/while/body/eval_jaxpr/all_to_all | solution.py:97
  289.4 6.1 collective-permute-start
  297.9 20.4 %all-to-all-start = ((bf16[16,3,4096]{2,1,0:T(4,128)(2,1)}), bf16[16,3,4096]{2,1,0:T(4,128)(2,1)}, u32[]{:S(2)}, u32[]{:S(2)}) async-start(bf16[16,3,4096]{2,1,0:T(4,128)(2,1)} %bitcast.91), calls=%async_computation | async-start | bytes 1048576 | tf_op jit(solution)/shard_map/while/body/eval_jaxpr/all_to_all | solution.py:97
  342.1 6.1 collective-permute-start
  350.5 20.4 %all-to-all-start = ((bf16[16,3,4096]{2,1,0:T(4,128)(2,1)}), bf16[16,3,4096]{2,1,0:T(4,128)(2,1)}, u32[]{:S(2)}, u32[]{:S(2)}) async-start(bf16[16,3,4096]{2,1,0:T(4,128)(2,1)} %bitcast.91), calls=%async_computation | async-start | bytes 1048576 | tf_op jit(solution)/shard_map/while/body/eval_jaxpr/all_to_all | solution.py:97
  394.7 6.1 collective-permute-start
  403.2 20.2 all-to-all-start
  447.2 8.4 collective-permute-start
  457.9 20.2 all-to-all-start
  501.8 8.6 collective-permute-start
  512.7 20.2 all-to-all-start
  556.6 8.6 collective-permute-start
  567.4 20.2 all-to-all-start
  611.3 8.6 collective-permute-start
  622.2 20.2 all-to-all-start
  666.1 8.6 collective-permute-start
  677.0 20.2 all-to-all-start
  720.9 8.6 collective-permute-start
  731.7 20.2 all-to-all-start
  775.6 8.6 collective-permute-start
  786.5 20.2 all-to-all-start
  830.4 8.6 collective-permute-start
  841.3 20.2 all-to-all-start
  885.2 8.6 collective-permute-start
  896.0 20.2 all-to-all-start
  939.9 8.6 collective-permute-start
  950.8 20.2 all-to-all-start
  972.0 85.5 %copy-start.9 = (bf16[16,8,8,3]{1,2,3,0:T(8,128)(2,1)S(1)}, bf16[16,8,8,3]{1,2,3,0:T(8,128)(2,1)}, u32[]{:S(2)}) copy-start(bf16[16,8,8,3]{1,2,3,0:T(8,128)(2,1)} %copy-done.8) | copy-start | bytes 18436 | tf_op jit(solution)/shard_map/while
  994.7 62.9 %collective-permute-start = (bf16[8,4096]{1,0:T(8,128)(2,1)S(1)}, bf16[8,4096]{1,0:T(8,128)(2,1)S(1)}, u32[]{:S(2)}, u32[]{:S(2)}) collective-permute-start(bf16[8,4096]{1,0:T(8,128)(2,1)S(1)} %get-tuple-element.441), channel_id=1, source_target_pairs={{16,0},{32,16},{48,32},{64,48},{80,64},{96,80},{112,96},{128,112},... | collective-permute-start | bytes 196616 | tf_op jit(solution)/shard_map/while/body/eval_jaxpr/ppermute | solution.py:13
  1059.8 20.2 all-to-all-start
  1109.7 8.6 collective-permute-start
  1120.6 20.2 all-to-all-start
  1170.5 8.5 collective-permute-start
  1181.3 20.2 all-to-all-start
  1231.3 8.6 collective-permute-start
  1242.1 20.2 all-to-all-start
  1292.0 8.6 collective-permute-start
  1302.9 20.2 all-to-all-start
  1352.8 8.5 collective-permute-start
  1363.6 20.2 all-to-all-start
  1413.6 8.6 collective-permute-start
  1424.5 20.2 all-to-all-start
  1474.4 8.6 collective-permute-start
  1485.2 20.2 all-to-all-start
  1535.1 8.5 collective-permute-start
  1545.9 20.2 all-to-all-start
  1595.9 8.6 collective-permute-start
  1606.8 20.2 all-to-all-start
  1656.7 8.5 collective-permute-start
  1667.5 20.2 all-to-all-start
  1717.4 8.6 collective-permute-start
  1728.2 20.2 all-to-all-start
  1778.2 8.6 collective-permute-start
  1789.1 20.2 all-to-all-start
  1839.0 8.5 collective-permute-start
  1849.8 20.2 all-to-all-start
  1899.7 8.6 collective-permute-start
  1910.6 20.2 all-to-all-start
  1960.5 8.6 collective-permute-start
  1971.4 20.2 all-to-all-start
  2021.3 6.1 collective-permute-start
  (130 other events, 2423.6 us)
where the time goes:
time: 2040 us; the launch traced here: 2030 us
  waiting for transfers between devices  854 us (42%)
  blocking collectives  636 us (31%)
  starting transfers between devices  226 us (11%)
  matrix products  160 us (8%)
  local copies, waits for them, and re-layouts  137 us (7%)
    all_to_all x31, blocking collectives, tick(): lax.all_to_all(back.reshape(expert_count, capacity, model_width), 'expert...  636 us
    all_to_all x31, waiting for transfers between devices, tick(): lax.all_to_all(grad_rows, 'expert', split_axis=0, concat_axis=0, tiled=True)  450 us
    ppermute x31, waiting for transfers between devices, passed_along(): return lax.ppermute(x, axis, pairs)  268 us
    all_to_all x31, starting transfers between devices, tick(): lax.all_to_all(grad_rows, 'expert', split_axis=0, concat_axis=0, tiled=True)  177 us
    all_to_all x1, waiting for transfers between devices, on_device(): lax.all_to_all(outgoing, 'expert', split_axis=1, concat_axis=1, tiled=True)  137 us
    dot_general x31, matrix products, tick(): jnp.einsum('tec,ekcd->td', combine_micro, returned, preferred_element_typ...  56.5 us
  transfers between devices with their start and end apart: 63, of which 63 were waited for; matrix products, arithmetic and copies ran while one was open for 0% of the time, Pallas kernels for 0%

commit v1 on v0

v1 whole, which is shorter than its diff:
```python
import jax
import jax.numpy as jnp
from jax import lax
from jax.experimental import pallas as pl
from jax.experimental.pallas import tpu as pltpu
from jax.sharding import PartitionSpec as P

EXPERTS = 8
CAP = 3
SLOTS = EXPERTS * CAP
MB = 16
TOK = 8
D = 4096
FOLD = 16
LANES = 128
HALF = FOLD * LANES
ROWS = CAP * FOLD
PAIR_ROWS = SLOTS * FOLD
TOK_ROWS = TOK * FOLD
PAD = 32
HID = 256
LAST = 15
FAR_FIRST = (4, 3, 5, 2, 6, 1, 7)
MESH = pl.DeviceIdType.MESH
BF16 = jnp.bfloat16
F32 = jnp.float32


def matmul(a, b):
    return lax.dot_general(a, b, (((1,), (0,)), ((), ())), preferred_element_type=F32)


def iota(shape, dim):
    return lax.broadcasted_iota(jnp.int32, shape, dim)


def chain_kernel(
    x_ref, og_ref, disp_ref, comb_ref, wg_hbm, wu_hbm, wd_hbm, wgt_hbm, wut_hbm,
    out_ref,
    wg, wu, wd, wgt, wut, comb_next,
    send_x, send_g, send_r, recv_x, recv_g, recv_r, recv_last,
    g_prev, g_here, saved, lhs, folded, unfold_mat, fold_mat,
    own_sems, swap_send, swap_recv, comb_send, comb_recv,
    x_send, g_send, r_send, p_send, o_send,
    x_recv, g_recv, r_recv, last_recv, p_recv, o_recv,
):
    s = lax.axis_index("section")
    i = lax.axis_index("expert")
    z = i // 2
    c = lax.rem(i, 2)
    up = lax.rem(s + 1, LAST + 1)
    down = lax.rem(s + LAST, LAST + 1)

    def at(section, chip):
        return {"section": section, "expert": chip * 2 + c}

    sibling = {"section": s, "expert": z * 2 + 1 - c}

    barrier = pltpu.get_barrier_semaphore()
    pl.semaphore_signal(barrier, inc=1, device_id=sibling, device_id_type=MESH)
    for d in range(1, EXPERTS):
        pl.semaphore_signal(barrier, inc=1, device_id=at(s, lax.rem(z + d, EXPERTS)), device_id_type=MESH)
    for d in range(EXPERTS):
        pl.semaphore_signal(barrier, inc=1, device_id=at(up, lax.rem(z + d, EXPERTS)), device_id_type=MESH)
        pl.semaphore_signal(barrier, inc=1, device_id=at(down, lax.rem(z + d, EXPERTS)), device_id_type=MESH)
    pl.semaphore_wait(barrier, 1 + 3 * EXPERTS - 1)

    weights = ((wg_hbm, wg), (wu_hbm, wu), (wd_hbm, wd), (wgt_hbm, wgt), (wut_hbm, wut))

    def own_copy(n):
        return pltpu.make_async_copy(weights[n][0], weights[n][1].at[c], own_sems.at[n])

    def swap_copy(n):
        return pltpu.make_async_remote_copy(
            src_ref=weights[n][0], dst_ref=weights[n][1].at[c], send_sem=swap_send.at[n],
            recv_sem=swap_recv.at[n], device_id=sibling, device_id_type=MESH,
        )

    def weights_ready(n):
        own_copy(n).wait()
        swap_copy(n).wait_recv()

    for n in range(5):
        swap_copy(n).start()
        own_copy(n).start()

    def comb_copy():
        return pltpu.make_async_remote_copy(
            src_ref=comb_ref, dst_ref=comb_next, send_sem=comb_send, recv_sem=comb_recv,
            device_id=at(down, z), device_id_type=MESH,
        )

    @pl.when(s > 0)
    def _():
        comb_copy().start()

    r0, r1 = iota((FOLD * PAD, PAIR_ROWS), 0), iota((FOLD * PAD, PAIR_ROWS), 1)
    hit = ((r0 & 31) == (r1 >> 4)) & ((r0 >> 5) == (r1 & 15))
    unfold_mat[...] = jnp.where(hit, 1.0, 0.0).astype(BF16)
    r0, r1 = iota((PAIR_ROWS, FOLD * PAD), 0), iota((PAIR_ROWS, FOLD * PAD), 1)
    hit = ((r1 & 31) == (r0 >> 4)) & ((r1 >> 5) == (r0 & 15))
    fold_mat[...] = jnp.where(hit, 1.0, 0.0).astype(BF16)

    def dispatch_matrix(m):
        rows = iota((PAIR_ROWS, PAD), 0) >> 4
        spread = jnp.where(rows == iota((PAIR_ROWS, PAD), 1), 1.0, 0.0).astype(BF16)
        wide = matmul(spread, disp_ref[m])
        same = (iota((PAIR_ROWS, TOK_ROWS), 0) & 15) == (iota((PAIR_ROWS, TOK_ROWS), 1) & 15)
        return jnp.where(same, wide, 0.0).astype(BF16)

    def combine_matrix(ref, m):
        columns = iota((LANES, PAIR_ROWS), 1) >> 4
        spread = jnp.where(columns == iota((LANES, PAIR_ROWS), 0), 1.0, 0.0).astype(BF16)
        wide = matmul(ref[m], spread)
        same = (iota((TOK_ROWS, PAIR_ROWS), 0) & 15) == (iota((TOK_ROWS, PAIR_ROWS), 1) & 15)
        return jnp.where(same, wide, 0.0).astype(BF16)

    def half(h):
        return pl.ds(h * ROWS, ROWS)

    def part(value):
        return value.astype(BF16).reshape(EXPERTS, ROWS, LANES)

    def spread_x(m):
        matrix = dispatch_matrix(m)
        for h in range(2):
            send_x[m, :, half(h), :] = part(matmul(matrix, x_ref[m, h]))
        for d in FAR_FIRST:
            to = lax.rem(z + d, EXPERTS)
            pltpu.make_async_remote_copy(
                src_ref=send_x.at[m, to], dst_ref=recv_x.at[m, z], send_sem=x_send,
                recv_sem=x_recv.at[m], device_id=at(s, to), device_id_type=MESH,
            ).start()
        pltpu.make_async_copy(send_x.at[m, z], recv_x.at[m, z], x_recv.at[m]).start()

    def spread_g(m, h, matrix, rows):
        send_g[m, :, half(h), :] = part(matmul(matrix, rows))
        for d in FAR_FIRST:
            to = lax.rem(z + d, EXPERTS)
            pltpu.make_async_remote_copy(
                src_ref=send_g.at[m, to, half(h)], dst_ref=recv_g.at[m, z, half(h)], send_sem=g_send,
                recv_sem=g_recv.at[m, h], device_id=at(s, to), device_id_type=MESH,
            ).start()
        pltpu.make_async_copy(
            send_g.at[m, z, half(h)], recv_g.at[m, z, half(h)], g_recv.at[m, h]
        ).start()

    def arrived(ref, m, h, sem):
        whole = ref.at[m, :, half(h)]
        pltpu.make_async_copy(whole, whole, sem.at[m, h]).wait()

    def unfold(ref, m, h):
        rows = matmul(unfold_mat[...], ref[m, :, half(h), :].reshape(PAIR_ROWS, LANES)).astype(BF16)
        for j in range(FOLD):
            lhs[:, h * HALF + j * LANES : h * HALF + (j + 1) * LANES] = rows[j * PAD : (j + 1) * PAD]

    def forward(m):
        pltpu.make_async_copy(recv_x.at[m], recv_x.at[m], x_recv.at[m]).wait()
        for h in range(2):
            unfold(recv_x, m, h)
        for k in range(2):
            gate = matmul(lhs[...], wg[k])
            value = matmul(lhs[...], wu[k])
            sig = jax.nn.sigmoid(gate)
            saved[m, 0, :, k * HID : (k + 1) * HID] = gate * sig
            saved[m, 1, :, k * HID : (k + 1) * HID] = value * (sig * (1.0 + gate * (1.0 - sig)))

    def send_back(m, h):
        @pl.when(s > 0)
        def _():
            for d in FAR_FIRST + (0,):
                to = lax.rem(z + d, EXPERTS)
                pltpu.make_async_remote_copy(
                    src_ref=send_r.at[m, to, half(h)], dst_ref=recv_r.at[m, z, half(h)], send_sem=r_send,
                    recv_sem=r_recv.at[m, h], device_id=at(down, to), device_id_type=MESH,
                ).start()

        @pl.when(s == 0)
        def _():
            for d in FAR_FIRST:
                to = lax.rem(z + d, EXPERTS)
                pltpu.make_async_remote_copy(
                    src_ref=send_r.at[m, to, half(h)], dst_ref=recv_last.at[m, z, half(h)], send_sem=r_send,
                    recv_sem=last_recv.at[m, h], device_id=at(s, to), device_id_type=MESH,
                ).start()
            pltpu.make_async_copy(
                send_r.at[m, z, half(h)], recv_last.at[m, z, half(h)], last_recv.at[m, h]
            ).start()

    def backward(m):
        sums = [None, None]
        for h in range(2):
            arrived(recv_g, m, h, g_recv)
            unfold(recv_g, m, h)
            columns = slice(h * HALF, (h + 1) * HALF)
            for k in range(2):
                term = matmul(lhs[:, columns], wd[k, columns, :])
                sums[k] = term if h == 0 else sums[k] + term
        pieces = []
        for k in range(2):
            hidden = slice(k * HID, (k + 1) * HID)
            pieces.append(
                ((sums[k] * saved[m, 1, :, hidden]).astype(BF16), (sums[k] * saved[m, 0, :, hidden]).astype(BF16))
            )
        width = 4 * LANES
        for h in range(2):
            for n in range(HALF // width):
                columns = slice(h * HALF + n * width, h * HALF + (n + 1) * width)
                total = matmul(pieces[0][0], wgt[0, :, columns])
                total += matmul(pieces[0][1], wut[0, :, columns])
                total += matmul(pieces[1][0], wgt[1, :, columns])
                total += matmul(pieces[1][1], wut[1, :, columns])
                rows = total.astype(BF16)
                for q in range(4):
                    j = n * 4 + q
                    folded[j * PAD : (j + 1) * PAD, :] = rows[:, q * LANES : (q + 1) * LANES]
            send_r[m, :, half(h), :] = part(matmul(fold_mat[...], folded[...]))
            send_back(m, h)

    def pass_on(m, h):
        pltpu.make_async_remote_copy(
            src_ref=g_here.at[m, h], dst_ref=out_ref.at[m, h], send_sem=o_send, recv_sem=o_recv,
            device_id=at(up, z), device_id_type=MESH,
        ).start()

        @pl.when(s > 0)
        def _():
            pltpu.make_async_remote_copy(
                src_ref=g_here.at[m, h], dst_ref=g_prev.at[m, h], send_sem=p_send,
                recv_sem=p_recv.at[m, h], device_id=at(down, z), device_id_type=MESH,
            ).start()

    def gather(m):
        dispatch = dispatch_matrix(m)
        combine = combine_matrix(comb_next, m)
        for h in range(2):
            @pl.when(s < LAST - 1)
            def _():
                pltpu.make_async_copy(g_prev.at[m, h], g_prev.at[m, h], p_recv.at[m, h]).wait()

            arrived(recv_r, m, h, r_recv)
            mixed = matmul(combine, recv_r[m, :, half(h), :].reshape(PAIR_ROWS, LANES))
            rows = (g_prev[m, h].astype(F32) + mixed).astype(BF16)
            g_here[m, h] = rows
            spread_g(m, h, dispatch, rows)
        for h in range(2):
            pass_on(m, h)

    def first_gather(m):
        matrix = dispatch_matrix(m)
        for h in range(2):
            spread_g(m, h, matrix, og_ref[m, h])

    def finish(m):
        combine = combine_matrix(comb_ref, m)
        for h in range(2):
            arrived(recv_last, m, h, last_recv)
            mixed = matmul(combine, recv_last[m, :, half(h), :].reshape(PAIR_ROWS, LANES))
            out_ref[m, h] = (g_here[m, h].astype(F32) + mixed).astype(BF16)

    ahead = jnp.minimum(MB, 1 + 4 * (LAST - s))
    x_ahead = jnp.minimum(MB, ahead + 1)

    spread_x(0)

    @pl.when(s == LAST)
    def _():
        first_gather(0)

    def more_x(m, carry):
        spread_x(m)
        return carry

    lax.fori_loop(1, x_ahead, more_x, 0)

    @pl.when(s == LAST - 1)
    def _():
        g_prev[...] = og_ref[...]

    weights_ready(0)
    weights_ready(1)

    def more_forward(m, carry):
        forward(m)
        return carry

    lax.fori_loop(0, ahead, more_forward, 0)
    weights_ready(2)
    weights_ready(3)
    weights_ready(4)

    @pl.when(s < LAST)
    def _():
        comb_copy().wait_recv()

    def step(m, carry):
        @pl.when(s < LAST)
        def _():
            gather(m)

        @pl.when((s == LAST) & (m + 1 < MB))
        def _():
            first_gather(m + 1)

        @pl.when(m + x_ahead < MB)
        def _():
            spread_x(m + x_ahead)

        backward(m)

        @pl.when(m + ahead < MB)
        def _():
            forward(m + ahead)

        @pl.when((s == 0) & (m > 0))
        def _():
            finish(m - 1)

        return carry

    lax.fori_loop(0, MB, step, 0)

    @pl.when(s == 0)
    def _():
        finish(MB - 1)

    for n in range(5):
        swap_copy(n).wait_send()

    def drain(ref, sem):
        pltpu.make_async_copy(ref, ref, sem).wait()

    drain(send_x.at[:, pl.ds(0, EXPERTS - 1)], x_send)
    drain(send_g.at[:, pl.ds(0, EXPERTS - 1)], g_send)

    @pl.when(s > 0)
    def _():
        comb_copy().wait_send()
        drain(send_r, r_send)
        drain(out_ref, o_recv)

    @pl.when(s == 0)
    def _():
        drain(send_r.at[:, pl.ds(0, EXPERTS - 1)], r_send)

    @pl.when(s < LAST)
    def _():
        drain(g_here, o_send)

    @pl.when((s > 0) & (s < LAST))
    def _():
        drain(g_here, p_send)


def chain(x, og, disp, comb, wg, wu, wd, wgt, wut):
    vmem = pl.BlockSpec(memory_space=pltpu.VMEM)
    anywhere = pl.BlockSpec(memory_space=pl.ANY)
    blocks = (MB, EXPERTS, 2 * ROWS, LANES)
    rows = (MB, 2, TOK_ROWS, LANES)
    dma = pltpu.SemaphoreType.DMA
    return pl.pallas_call(
        chain_kernel,
        out_shape=jax.ShapeDtypeStruct(rows, BF16),
        in_specs=[vmem] * 4 + [anywhere] * 5,
        out_specs=vmem,
        scratch_shapes=[
            pltpu.VMEM((2, D, HID), BF16),
            pltpu.VMEM((2, D, HID), BF16),
            pltpu.VMEM((2, D, HID), BF16),
            pltpu.VMEM((2, HID, D), BF16),
            pltpu.VMEM((2, HID, D), BF16),
            pltpu.VMEM((MB, TOK_ROWS, LANES), BF16),
        ]
        + [pltpu.VMEM(blocks, BF16)] * 7
        + [
            pltpu.VMEM(rows, BF16),
            pltpu.VMEM(rows, BF16),
            pltpu.VMEM((MB, 2, PAD, 2 * HID), F32),
            pltpu.VMEM((PAD, D), BF16),
            pltpu.VMEM((FOLD * PAD, LANES), BF16),
            pltpu.VMEM((FOLD * PAD, PAIR_ROWS), BF16),
            pltpu.VMEM((PAIR_ROWS, FOLD * PAD), BF16),
            dma((5,)),
            dma((5,)),
            dma((5,)),
            dma,
            dma,
            dma,
            dma,
            dma,
            dma,
            dma,
            dma((MB,)),
            dma((MB, 2)),
            dma((MB, 2)),
            dma((MB, 2)),
            dma((MB, 2)),
            dma,
        ],
        compiler_params=pltpu.CompilerParams(
            collective_id=0, has_side_effects=True, vmem_limit_bytes=60 * 1024 * 1024
        ),
    )(x, og, disp, comb, wg, wu, wd, wgt, wut)


def fold_rows(x):
    return x.reshape(MB, TOK, 2, FOLD, LANES).transpose(0, 2, 1, 3, 4).reshape(MB, 2, TOK_ROWS, LANES)


def on_device(layer_inputs, expert_ids, gates, w_gate, w_up, w_down, out_grad):
    pairs = expert_ids[0].reshape(MB, TOK * 2)
    token = jnp.arange(TOK * 2, dtype=jnp.int32) // 2
    same = (pairs[:, :, None] == pairs[:, None, :]) & (token[None, :] < token[:, None])[None]
    slot = jnp.sum(same.astype(jnp.int32), axis=-1)
    target = jnp.repeat((pairs * CAP + slot).reshape(MB, TOK, 2), FOLD, axis=1)
    gate = jnp.repeat(gates[0], FOLD, axis=1)
    down = jnp.arange(PAD, dtype=jnp.int32)[None, :, None]
    across = jnp.arange(LANES, dtype=jnp.int32)[None, None, :]
    disp = ((target[:, None, :, 0] == down) | (target[:, None, :, 1] == down)).astype(BF16)
    zero = jnp.zeros((), BF16)
    comb = jnp.where(
        target[:, :, 0:1] == across, gate[:, :, 0:1],
        jnp.where(target[:, :, 1:2] == across, gate[:, :, 1:2], zero),
    )
    out = chain(
        fold_rows(layer_inputs[0]), fold_rows(out_grad), disp, comb,
        w_gate[0], w_up[0], w_down[0].T, w_gate[0].T, w_up[0].T,
    )
    out = out.reshape(MB, 2, TOK, FOLD, LANES).transpose(0, 2, 1, 3, 4).reshape(MB, TOK, D)
    return out[None]


def solution(mesh):
    placed = (
        P("section", None, "expert", None),
        P("section", None, "expert", None),
        P("section", None, "expert", None),
        P("section", None, "expert"),
        P("section", None, "expert"),
        P("section", "expert", None),
        P(None, "expert", None),
    )
    return jax.shard_map(
        on_device,
        mesh=mesh,
        in_specs=placed,
        out_specs=P("section", None, "expert", None),
        check_vma=False,
    )
```

time: 2040 us -> 487 us (0.24)
  waiting for transfers between devices: 854 us -> 0 us
  blocking collectives: 636 us -> 0 us
  Pallas kernels: 0 us -> 462 us
  starting transfers between devices: 226 us -> 0 us
  matrix products: 160 us -> 0 us
  local copies, waits for them, and re-layouts: 137 us -> 19.5 us
    all_to_all x31 -> x0, blocking collectives: 636 us -> none  [tick(): lax.all_to_all(back.reshape(expert_count, capacity, model_width), 'expert...]
    all_to_all x32 -> x0, waiting for transfers between devices: 586 us -> none  [the longest x31 450 us: tick(): lax.all_to_all(grad_rows, 'expert', split_axis=0, concat_axis=0, tiled=True)]
    pallas_call x0 -> x1, Pallas kernels: none -> 462 us  [chain(): pl.pallas_call(chain_kernel, out_shape=jax.ShapeDtypeStruct(rows, BF16),...]
    ppermute x31 -> x0, waiting for transfers between devices: 268 us -> none  [passed_along(): return lax.ppermute(x, axis, pairs)]
    all_to_all x32 -> x0, starting transfers between devices: 186 us -> none  [the longest x31 177 us: tick(): lax.all_to_all(grad_rows, 'expert', split_axis=0, concat_axis=0, tiled=True)]
    dot_general x113 -> x0, matrix products: 160 us -> none  [the longest x31 56.5 us: tick(): jnp.einsum('tec,ekcd->td', combine_micro, returned, preferred_element_typ...]
    reshape x48 -> x3, local copies, waits for them, and re-layouts: 68 us -> 1.44 us  [the longest x1 1.23 us: fold_rows(): x.reshape(MB, TOK, 2, FOLD, LANES).transpose(0, 2, 1, 3, 4)]
    ppermute x31 -> x0, starting transfers between devices: 39.7 us -> none  [passed_along(): return lax.ppermute(x, axis, pairs)]
  transfers between devices with their start and end apart: 63 -> 0, of which waited for: 63 -> 0; matrix products, arithmetic and copies ran while one was open for 0% -> 0% of each run, Pallas kernels for 0% -> 0%
where the time goes in v1:
time: 487 us; the launch traced here: 486 us
  Pallas kernels  462 us (95%)
  local copies, waits for them, and re-layouts  19.5 us (4%)
    pallas_call x1, Pallas kernels, chain(): pl.pallas_call(chain_kernel, out_shape=jax.ShapeDtypeStruct(rows, BF16),...  462 us
    unnamed x7, local copies, waits for them, and re-layouts  11.2 us

profile of v1, /device:TPU:32, one launch (start us, length us, event | category | flops | bytes accessed | tf_op | source)
XLA Modules:
  0.0 486.3 jit_solution(6383832211869502252)
XLA Ops:
  0.0 0.0 copy-start.1
  0.0 0.1 broadcast_compare_fusion
  0.1 0.8 copy.39
  0.9 0.8 copy.35
  1.7 0.4 convert_reduce_fusion
  2.1 0.1 copy.37
  2.2 0.7 bitcast_add_fusion
  2.9 0.1 copy.38
  3.0 0.1 broadcast_in_dim.36
  3.1 0.1 reshape.84
  3.2 0.1 broadcast_in_dim.35
  3.3 0.1 reshape.83
  3.4 0.7 fusion.3.disp_ref
  4.1 2.3 fusion.comb_ref
  6.5 2.4 copy.33
  8.9 0.0 copy-done.1
  8.9 1.2 copy.34
  10.1 0.0 copy-start
  10.1 4.2 copy.42
  14.4 0.0 copy-done
  14.4 2.9 copy.40
  17.3 4.1 copy.41
  21.4 462.5 %shard_map.73 = bf16[16,2,128,128]{3,2,1,0:T(8,128)(2,1)} custom-call(bf16[16,2,128,128]{3,2,1,0:T(8,128)(2,1)} %bitcast.50, bf16[16,2,128,128]{3,2,1,0:T(8,128)(2,1)} %bitcast.51, bf16[16,32,128]{2,1,0:T(8,128)(2,1)} %fusion.3.disp_ref, bf16[16,128,128]{2,1,0:T(8,128)(2,1)} %fusion.comb_ref, bf16[4096,256]{1,0:T(8,128)(2,1)} %bitcast.44, ...), custom_call_target="tpu_custom_call" | custom-call | tf_op jit(solution)/shard_map/pallas_call | solution.py:361
  483.8 2.5 copy.45
  (3 shorter events, 0.0 us)
Async XLA Ops:
  0.0 8.9 %copy-start.1 = (bf16[16,8,4096]{2,1,0:T(8,128)(2,1)S(1)}, bf16[16,8,4096]{2,1,0:T(8,128)(2,1)}, u32[]{:S(2)}) copy-start(bf16[16,8,4096]{2,1,0:T(8,128)(2,1)} %param.13) | copy-start | bytes 3145732
  10.1 4.2 copy-start

commit v2 on v1

v2 whole, which is shorter than its diff:
```python
import jax
import jax.numpy as jnp
from jax import lax
from jax.experimental import pallas as pl
from jax.experimental.pallas import tpu as pltpu
from jax.sharding import PartitionSpec as P

EXPERTS = 8
CAP = 3
SLOTS = EXPERTS * CAP
MB = 16
PAIRS = MB // 2
TOK = 8
D = 4096
FOLD = 16
LANES = 128
HALF = FOLD * LANES
ROWS = CAP * FOLD
PAIR_ROWS = SLOTS * FOLD
TOK_ROWS = TOK * FOLD
PAD = 32
HID = 256
LINES = 16
LAST = LINES - 1
FIRST = 3
FAR_FIRST = (4, 3, 5, 2, 6, 1, 7)
MESH = pl.DeviceIdType.MESH
BF16 = jnp.bfloat16
F32 = jnp.float32


def matmul(a, b):
    return lax.dot_general(a, b, (((1,), (0,)), ((), ())), preferred_element_type=F32)


def iota(shape, dim):
    return lax.broadcasted_iota(jnp.int32, shape, dim)


def chain_kernel(
    x_ref, og_ref, pairs_ref, wg_hbm, wu_hbm, wd_hbm,
    out_ref,
    wg, wu, wd, wgt, wut, wd_raw, info, comb_info, top_info, x_help,
    send_x, send_g, send_r, recv_x, recv_g, recv_r, recv_last,
    g_prev, g_here, saved, lhs, folded, unfold_mat, fold_mat,
    own_sems, swap_send, swap_recv, info_send, info_recv, help_send, help_recv,
    x_send, g_send, r_send, p_send, o_send,
    x_recv, g_recv, r_recv, last_recv, p_recv, o_recv, turn,
):
    line = lax.axis_index("section")
    i = lax.axis_index("expert")
    z = i // 2
    c = lax.rem(i, 2)

    def off(by):
        return lax.rem(line + by, LINES)

    def at(section, chip):
        return {"section": section, "expert": chip * 2 + c}

    def other(d):
        return lax.rem(z + d, EXPERTS)

    first = line == FIRST
    top = line == LAST
    helped = (line >= 12) & (line < LAST)
    helper = line < 3
    sibling = {"section": line, "expert": z * 2 + 1 - c}
    barrier = pltpu.get_barrier_semaphore()

    def greet(device):
        pl.semaphore_signal(barrier, inc=1, device_id=device, device_id_type=MESH)

    greet(sibling)
    for d in range(1, EXPERTS):
        greet(at(line, other(d)))
    for d in range(EXPERTS):
        greet(at(off(1), other(d)))
        greet(at(off(15), other(d)))

    @pl.when(top)
    def _():
        for d in range(EXPERTS):
            greet(at(FIRST, other(d)))

    @pl.when(first)
    def _():
        for d in range(EXPERTS):
            greet(at(LAST, other(d)))

    @pl.when(helped)
    def _():
        for d in range(EXPERTS):
            greet(at(off(4), other(d)))

    @pl.when(helper)
    def _():
        greet(at(off(12), z))

    raw = ((wg_hbm, wg.at[c]), (wu_hbm, wu.at[c]), (wd_hbm, wd_raw))

    def own_copy(n):
        return pltpu.make_async_copy(raw[n][0], raw[n][1], own_sems.at[n])

    for n in (2, 0, 1):
        own_copy(n).start()

    whole = (wg, wu, wd, wgt, wut)

    def swap_copy(n):
        return pltpu.make_async_remote_copy(
            src_ref=whole[n].at[c], dst_ref=whole[n].at[c], send_sem=swap_send.at[n],
            recv_sem=swap_recv.at[n], device_id=sibling, device_id_type=MESH,
        )

    ids = (pairs_ref[0], pairs_ref[1])
    token = iota((MB, LANES), 1) & 7
    slots = [jnp.zeros((MB, LANES), F32), jnp.zeros((MB, LANES), F32)]
    for r in range(1, TOK):
        for k in range(2):
            earlier = pltpu.roll(ids[k], r, 1)
            for q in range(2):
                slots[q] += jnp.where((earlier == ids[q]) & (token >= r), 1.0, 0.0)
    for q in range(2):
        info[q] = ids[q] * CAP + slots[q]
        info[2 + q] = pairs_ref[2 + q]

    r0, r1 = iota((FOLD * PAD, PAIR_ROWS), 0), iota((FOLD * PAD, PAIR_ROWS), 1)
    hit = ((r0 & 31) == (r1 >> 4)) & ((r0 >> 5) == (r1 & 15))
    unfold_mat[...] = jnp.where(hit, 1.0, 0.0).astype(BF16)
    r0, r1 = iota((PAIR_ROWS, FOLD * PAD), 0), iota((PAIR_ROWS, FOLD * PAD), 1)
    hit = ((r1 & 31) == (r0 >> 4)) & ((r1 >> 5) == (r0 & 15))
    fold_mat[...] = jnp.where(hit, 1.0, 0.0).astype(BF16)

    extra = jnp.where(top | first | helper, EXPERTS, jnp.where(helped, 1, 0))
    pl.semaphore_wait(barrier, 3 * EXPERTS + extra)

    def info_copy(n):
        return pltpu.make_async_remote_copy(
            src_ref=info, dst_ref=(comb_info, top_info, top_info)[n], send_sem=info_send.at[n],
            recv_sem=info_recv.at[n], device_id=at((off(15), FIRST, off(4))[n], z), device_id_type=MESH,
        )

    @pl.when(line > 0)
    def _():
        info_copy(0).start()

    @pl.when(top)
    def _():
        info_copy(1).start()

    @pl.when(helped)
    def _():
        info_copy(2).start()

    def matrix(ref, m, first, second):
        place = (iota((PAIR_ROWS, TOK_ROWS), 0) >> 4).astype(F32)
        same = (iota((PAIR_ROWS, TOK_ROWS), 0) & 15) == (iota((PAIR_ROWS, TOK_ROWS), 1) >> 3)
        row = pl.ds(m, 1)
        value = jnp.where(ref[0, row] == place, first, jnp.where(ref[1, row] == place, second, 0.0))
        return jnp.where(same, value, 0.0)

    def dispatch_matrix(ref, m):
        return matrix(ref, m, 1.0, 1.0).astype(BF16)

    def combine_matrix(ref, m):
        row = pl.ds(m, 1)
        return matrix(ref, m, ref[2, row], ref[3, row]).T.astype(BF16)

    def half(h):
        return pl.ds(h * ROWS, ROWS)

    def part(value):
        return value.astype(BF16).reshape(EXPERTS, ROWS, LANES)

    def fold_pair(ref, p):
        both = ref[pl.ds(pl.multiple_of(p * 2 * TOK, 2 * TOK), 2 * TOK), :].astype(F32)
        result = []
        for b in range(2):
            rows = both[b * TOK : (b + 1) * TOK]
            halves = []
            for h in range(2):
                columns = [rows[:, h * HALF + j * LANES : h * HALF + (j + 1) * LANES] for j in range(FOLD)]
                halves.append(jnp.concatenate(columns, axis=0).astype(BF16))
            result.append(halves)
        return result

    def fill_x(ref, p, from_info):
        values = fold_pair(ref, p)
        for b in range(2):
            dispatch = dispatch_matrix(from_info, p * 2 + b)
            for h in range(2):
                send_x[p, :, pl.ds((b * 2 + h) * ROWS, ROWS), :] = part(matmul(dispatch, values[b][h]))

    def x_copy(p, to, to_line):
        return pltpu.make_async_remote_copy(
            src_ref=send_x.at[p, to], dst_ref=recv_x.at[p, z], send_sem=x_send,
            recv_sem=x_recv.at[p], device_id=at(to_line, to), device_id_type=MESH,
        )

    def pair_rows(p):
        return pl.ds(pl.multiple_of(p * 2 * TOK, 2 * TOK), 2 * TOK)

    def help_copy(p):
        return pltpu.make_async_remote_copy(
            src_ref=x_ref.at[pair_rows(p)], dst_ref=x_help.at[pair_rows(p)], send_sem=help_send,
            recv_sem=help_recv.at[p], device_id=at(off(4), z), device_id_type=MESH,
        )

    def spread_x(p):
        fill_x(x_ref, p, info)
        for d in FAR_FIRST:
            x_copy(p, other(d), line).start()
        pltpu.make_async_copy(send_x.at[p, z], recv_x.at[p, z], x_recv.at[p]).start()

    def g_copy(m, h, to, to_line):
        return pltpu.make_async_remote_copy(
            src_ref=send_g.at[m, to, half(h)], dst_ref=recv_g.at[m, z, half(h)], send_sem=g_send,
            recv_sem=g_recv.at[m, h], device_id=at(to_line, to), device_id_type=MESH,
        )

    def spread_g(m, h, dispatch, rows):
        send_g[m, :, half(h), :] = part(matmul(dispatch, rows))
        for d in FAR_FIRST:
            g_copy(m, h, other(d), line).start()
        pltpu.make_async_copy(
            send_g.at[m, z, half(h)], recv_g.at[m, z, half(h)], g_recv.at[m, h]
        ).start()

    def spread_top(m, h, dispatch, rows):
        send_g[m, :, half(h), :] = part(matmul(dispatch, rows))
        for d in FAR_FIRST + (0,):
            g_copy(m, h, other(d), LAST).start()

    def arrived(ref, m, h, sem):
        block = ref.at[m, :, half(h)]
        pltpu.make_async_copy(block, block, sem.at[m, h]).wait()

    def drain(ref, sem):
        pltpu.make_async_copy(ref, ref, sem).wait()

    def unfold(rows, b, h):
        rows = matmul(unfold_mat[...], rows.reshape(PAIR_ROWS, LANES)).astype(BF16)
        for j in range(FOLD):
            columns = slice(h * HALF + j * LANES, h * HALF + (j + 1) * LANES)
            lhs[b * PAD : (b + 1) * PAD, columns] = rows[j * PAD : (j + 1) * PAD]

    def forward(p):
        drain(recv_x.at[p], x_recv.at[p])
        for b in range(2):
            for h in range(2):
                unfold(recv_x[p, :, pl.ds((b * 2 + h) * ROWS, ROWS), :], b, h)
        for k in range(2):
            hidden = slice(k * HID, (k + 1) * HID)
            gate = matmul(lhs[...], wg[k])
            value = matmul(lhs[...], wu[k])
            sig = jax.nn.sigmoid(gate)
            act = gate * sig
            coef = value * (sig * (1.0 + gate * (1.0 - sig)))
            for b in range(2):
                saved[p * 2 + b, 0, :, hidden] = act[b * PAD : (b + 1) * PAD]
                saved[p * 2 + b, 1, :, hidden] = coef[b * PAD : (b + 1) * PAD]

    def send_back(m, h):
        @pl.when(line > 0)
        def _():
            for d in FAR_FIRST + (0,):
                to = other(d)
                pltpu.make_async_remote_copy(
                    src_ref=send_r.at[m, to, half(h)], dst_ref=recv_r.at[m, z, half(h)], send_sem=r_send,
                    recv_sem=r_recv.at[m, h], device_id=at(off(15), to), device_id_type=MESH,
                ).start()

        @pl.when(line == 0)
        def _():
            for d in FAR_FIRST:
                to = other(d)
                pltpu.make_async_remote_copy(
                    src_ref=send_r.at[m, to, half(h)], dst_ref=recv_last.at[m, z, half(h)], send_sem=r_send,
                    recv_sem=last_recv.at[m, h], device_id=at(line, to), device_id_type=MESH,
                ).start()
            pltpu.make_async_copy(
                send_r.at[m, z, half(h)], recv_last.at[m, z, half(h)], last_recv.at[m, h]
            ).start()

    def backward(m):
        sums = [None, None]
        for h in range(2):
            arrived(recv_g, m, h, g_recv)
            unfold(recv_g[m, :, half(h), :], 0, h)
            columns = slice(h * HALF, (h + 1) * HALF)
            for k in range(2):
                term = matmul(lhs[:PAD, columns], wd[k, columns, :])
                sums[k] = term if h == 0 else sums[k] + term

        @pl.when((line < LAST) & (c == 0))
        def _():
            pl.semaphore_signal(turn, inc=1, device_id=sibling, device_id_type=MESH)

        pieces = []
        for k in range(2):
            hidden = slice(k * HID, (k + 1) * HID)
            pieces.append(
                ((sums[k] * saved[m, 1, :, hidden]).astype(BF16), (sums[k] * saved[m, 0, :, hidden]).astype(BF16))
            )
        width = 4 * LANES
        for h in range(2):
            for n in range(HALF // width):
                columns = slice(h * HALF + n * width, h * HALF + (n + 1) * width)
                total = matmul(pieces[0][0], wgt[0, :, columns])
                total += matmul(pieces[0][1], wut[0, :, columns])
                total += matmul(pieces[1][0], wgt[1, :, columns])
                total += matmul(pieces[1][1], wut[1, :, columns])
                rows = total.astype(BF16)
                for q in range(4):
                    j = n * 4 + q
                    folded[j * PAD : (j + 1) * PAD, :] = rows[:, q * LANES : (q + 1) * LANES]
            send_r[m, :, half(h), :] = part(matmul(fold_mat[...], folded[...]))
            send_back(m, h)

    def home(m):
        dispatch = dispatch_matrix(info, m)
        combine = combine_matrix(comb_info, m)

        @pl.when(c == 1)
        def _():
            pl.semaphore_wait(turn, 1)

        for h in range(2):
            @pl.when(line < LAST - 1)
            def _():
                drain(g_prev.at[m, h], p_recv.at[m, h])

            arrived(recv_r, m, h, r_recv)
            mixed = matmul(combine, recv_r[m, :, half(h), :].reshape(PAIR_ROWS, LANES))
            rows = (g_prev[m, h].astype(F32) + mixed).astype(BF16)
            g_here[m, h] = rows
            spread_g(m, h, dispatch, rows)

    def pass_on(m):
        @pl.when(line > 0)
        def _():
            for h in range(2):
                pltpu.make_async_remote_copy(
                    src_ref=g_here.at[m, h], dst_ref=g_prev.at[m, h], send_sem=p_send,
                    recv_sem=p_recv.at[m, h], device_id=at(off(15), z), device_id_type=MESH,
                ).start()

        pltpu.make_async_remote_copy(
            src_ref=g_here.at[m], dst_ref=out_ref.at[m], send_sem=o_send, recv_sem=o_recv,
            device_id=at(off(1), z), device_id_type=MESH,
        ).start()

    def finish(m):
        combine = combine_matrix(info, m)
        for h in range(2):
            arrived(recv_last, m, h, last_recv)
            mixed = matmul(combine, recv_last[m, :, half(h), :].reshape(PAIR_ROWS, LANES))
            out_ref[m, h] = (g_here[m, h].astype(F32) + mixed).astype(BF16)

    def loop(low, high, body):
        def run(n, carry):
            body(n)
            return carry

        lax.fori_loop(low, high, run, 0)

    @pl.when(line >= 12)
    def _():
        spread_x(0)

    @pl.when(helped)
    def _():
        loop(1, PAIRS, lambda p: help_copy(p).start())

    own_copy(0).wait()
    swap_copy(0).start()
    own_copy(1).wait()
    swap_copy(1).start()

    @pl.when(first)
    def _():
        info_copy(1).wait_recv()

        def start(p):
            values = fold_pair(og_ref, p)
            for b in range(2):
                dispatch = dispatch_matrix(top_info, p * 2 + b)
                for h in range(2):
                    spread_top(p * 2 + b, h, dispatch, values[b][h])

        loop(0, PAIRS, start)

    own_copy(2).wait()

    def turn_down(n):
        columns = pl.ds(pl.multiple_of(n * HID, HID), HID)
        wd[c, columns, :] = wd_raw[:, columns].T

    loop(0, D // HID, turn_down)
    swap_copy(2).start()

    def turn_up(n):
        rows = pl.ds(pl.multiple_of(n * HID, HID), HID)
        wgt[c, :, rows] = wg[c, rows, :].T
        wut[c, :, rows] = wu[c, rows, :].T

    loop(0, D // HID, turn_up)
    swap_copy(3).start()
    swap_copy(4).start()

    @pl.when(helper)
    def _():
        info_copy(2).wait_recv()

        def start(p):
            drain(x_help.at[pair_rows(p)], help_recv.at[p])
            fill_x(x_help, p, top_info)
            for d in FAR_FIRST + (0,):
                x_copy(p, other(d), off(12)).start()
            drain(send_x.at[p], x_send)

        loop(1, PAIRS, start)

    @pl.when(line == LAST - 1)
    def _():
        def start(p):
            values = fold_pair(og_ref, p)
            for b in range(2):
                for h in range(2):
                    g_prev[p * 2 + b, h] = values[b][h]

        loop(0, PAIRS, start)

    @pl.when(first)
    def _():
        drain(send_g, g_send)

    ahead = jnp.where(helped, 1 + LAST - line, jnp.minimum(PAIRS, 1 + 2 * (LAST - line)))
    x_ahead = jnp.minimum(PAIRS, ahead + 1)
    loop(jnp.where(line >= 12, 1, 0), jnp.where(helped, 1, x_ahead), spread_x)
    swap_copy(0).wait_recv()
    swap_copy(1).wait_recv()
    loop(0, ahead, forward)
    for n in (2, 3, 4):
        swap_copy(n).wait_recv()

    @pl.when(line < LAST)
    def _():
        info_copy(0).wait_recv()

    def step(n):
        @pl.when(line < LAST)
        def _():
            home(n)
            pass_on(n)

        k = n // 2

        @pl.when(top & (lax.rem(n, 2) == 0) & (k + x_ahead < PAIRS))
        def _():
            spread_x(k + x_ahead)

        @pl.when((lax.rem(n, 2) == 1) & (k + ahead < PAIRS))
        def _():
            forward(k + ahead)

        @pl.when((line == 0) & (n > 0))
        def _():
            finish(n - 1)

        backward(n)

    loop(0, MB, step)

    @pl.when(line == 0)
    def _():
        finish(MB - 1)

    for n in range(5):
        swap_copy(n).wait_send()

    @pl.when(helped)
    def _():
        info_copy(2).wait_send()
        drain(send_x.at[0, pl.ds(0, EXPERTS - 1)], x_send)
        drain(x_ref.at[pl.ds(2 * TOK, (PAIRS - 1) * 2 * TOK)], help_send)

    @pl.when(jnp.logical_not(helped))
    def _():
        drain(send_x.at[:, pl.ds(0, EXPERTS - 1)], x_send)

    @pl.when(line > 0)
    def _():
        info_copy(0).wait_send()
        drain(send_r, r_send)
        drain(out_ref, o_recv)

    @pl.when(line == 0)
    def _():
        drain(send_r.at[:, pl.ds(0, EXPERTS - 1)], r_send)

    @pl.when(top)
    def _():
        info_copy(1).wait_send()

    @pl.when(line < LAST)
    def _():
        drain(send_g.at[:, pl.ds(0, EXPERTS - 1)], g_send)
        drain(g_here, o_send)

    @pl.when((line > 0) & (line < LAST))
    def _():
        drain(g_here, p_send)


def chain(x, og, pairs, wg, wu, wd):
    vmem = pl.BlockSpec(memory_space=pltpu.VMEM)
    anywhere = pl.BlockSpec(memory_space=pl.ANY)
    x_blocks = (PAIRS, EXPERTS, 4 * ROWS, LANES)
    blocks = (MB, EXPERTS, 2 * ROWS, LANES)
    rows = (MB, 2, TOK_ROWS, LANES)
    dma = pltpu.SemaphoreType.DMA
    return pl.pallas_call(
        chain_kernel,
        out_shape=jax.ShapeDtypeStruct(rows, BF16),
        in_specs=[vmem] * 3 + [anywhere] * 3,
        out_specs=vmem,
        scratch_shapes=[pltpu.VMEM((2, D, HID), BF16)] * 3
        + [pltpu.VMEM((2, HID, D), BF16)] * 2
        + [pltpu.VMEM((HID, D), BF16)]
        + [pltpu.VMEM((4, MB, LANES), F32)] * 3
        + [pltpu.VMEM((MB * TOK, D), BF16)]
        + [pltpu.VMEM(x_blocks, BF16)]
        + [pltpu.VMEM(blocks, BF16)] * 2
        + [pltpu.VMEM(x_blocks, BF16)]
        + [pltpu.VMEM(blocks, BF16)] * 3
        + [pltpu.VMEM(rows, BF16)] * 2
        + [
            pltpu.VMEM((MB, 2, PAD, 2 * HID), F32),
            pltpu.VMEM((2 * PAD, D), BF16),
            pltpu.VMEM((FOLD * PAD, LANES), BF16),
            pltpu.VMEM((FOLD * PAD, PAIR_ROWS), BF16),
            pltpu.VMEM((PAIR_ROWS, FOLD * PAD), BF16),
        ]
        + [dma((3,)), dma((5,)), dma((5,)), dma((3,)), dma((3,)), dma, dma((PAIRS,))]
        + [dma] * 5
        + [dma((PAIRS,)), dma((MB, 2)), dma((MB, 2)), dma((MB, 2)), dma((MB, 2)), dma]
        + [pltpu.SemaphoreType.REGULAR],
        compiler_params=pltpu.CompilerParams(
            collective_id=0, has_side_effects=True, vmem_limit_bytes=60 * 1024 * 1024
        ),
    )(x, og, pairs, wg, wu, wd)


def on_device(layer_inputs, expert_ids, gates, w_gate, w_up, w_down, out_grad):
    pairs = jnp.concatenate([expert_ids[0].astype(F32), gates[0].astype(F32)], axis=-1)
    pairs = jnp.tile(pairs.transpose(2, 0, 1), (1, 1, FOLD))
    out = chain(
        layer_inputs.reshape(MB * TOK, D), out_grad.reshape(MB * TOK, D), pairs,
        w_gate[0], w_up[0], w_down[0],
    )
    out = out.reshape(MB, 2, FOLD, TOK, LANES).transpose(0, 3, 1, 2, 4).reshape(MB, TOK, D)
    return out[None]


def solution(mesh):
    placed = (
        P("section", None, "expert", None),
        P("section", None, "expert", None),
        P("section", None, "expert", None),
        P("section", None, "expert"),
        P("section", None, "expert"),
        P("section", "expert", None),
        P(None, "expert", None),
    )
    return jax.shard_map(
        on_device,
        mesh=mesh,
        in_specs=placed,
        out_specs=P("section", None, "expert", None),
        check_vma=False,
    )
```

time: 487 us -> 450 us (0.924); the launches traced: 486 us -> 442 us
  Pallas kernels: 462 us -> 438 us
  local copies, waits for them, and re-layouts: 19.5 us -> 3.03 us
    pallas_call x1, Pallas kernels: 462 us -> 438 us  [chain(): pl.pallas_call(chain_kernel, out_shape=jax.ShapeDtypeStruct(rows, BF16),...]
    unnamed x7 -> x1, local copies, waits for them, and re-layouts: 11.2 us -> 2.29 us
where the time goes in v2:
time: 450 us; the launch traced here: 442 us
  Pallas kernels  438 us (97%)
    pallas_call x1, Pallas kernels, chain(): pl.pallas_call(chain_kernel, out_shape=jax.ShapeDtypeStruct(rows, BF16),...  438 us

profile of v2, /device:TPU:32, one launch (start us, length us, event | category | flops | bytes accessed | tf_op | source)
XLA Modules:
  0.0 442.1 jit_solution(16403318973523615574)
XLA Ops:
  0.0 0.7 convert_bitcast_fusion
  0.7 0.7 bitcast_convert_fusion
  1.4 0.7 copy.10.pairs_ref
  2.2 437.6 %shard_map.73 = bf16[16,2,128,128]{3,2,1,0:T(8,128)(2,1)} custom-call(bf16[128,4096]{1,0:T(8,128)(2,1)} %bitcast.23, bf16[128,4096]{1,0:T(8,128)(2,1)} %bitcast.24, f32[4,16,128]{2,1,0:T(8,128)} %copy.10.pairs_ref, bf16[4096,256]{1,0:T(8,128)(2,1)} %bitcast.20, bf16[4096,256]{1,0:T(8,128)(2,1)} %bitcast.21, bf16[256,4096]{1,0:T(8,128)(2,1)} %bitcast.22), custom_call_target="tpu_custom_call" | custom-call | tf_op jit(solution)/shard_map/pallas_call | solution.py:524
  439.8 2.3 copy.12
  (3 shorter events, 0.0 us)

commit v3 on v2

--- a/solution.py
+++ b/solution.py
@@ -42,7 +42,7 @@
     out_ref,
     wg, wu, wd, wgt, wut, wd_raw, info, comb_info, top_info, x_help,
     send_x, send_g, send_r, recv_x, recv_g, recv_r, recv_last,
-    g_prev, g_here, saved, lhs, folded, unfold_mat, fold_mat,
+    g_prev, g_here, saved, lhs, folded, unfold_mat, fold_mat, dispatch_mat, combine_mat,
     own_sems, swap_send, swap_recv, info_send, info_recv, help_send, help_recv,
     x_send, g_send, r_send, p_send, o_send,
     x_recv, g_recv, r_recv, last_recv, p_recv, o_recv, turn,
@@ -287,16 +287,16 @@
         sums = [None, None]
         for h in range(2):
             arrived(recv_g, m, h, g_recv)
+            if h == 0:
+                @pl.when((line < LAST) & (c == 0))
+                def _():
+                    pl.semaphore_signal(turn, inc=1, device_id=sibling, device_id_type=MESH)
+
             unfold(recv_g[m, :, half(h), :], 0, h)
             columns = slice(h * HALF, (h + 1) * HALF)
             for k in range(2):
                 term = matmul(lhs[:PAD, columns], wd[k, columns, :])
                 sums[k] = term if h == 0 else sums[k] + term
-
-        @pl.when((line < LAST) & (c == 0))
-        def _():
-            pl.semaphore_signal(turn, inc=1, device_id=sibling, device_id_type=MESH)
-
         pieces = []
         for k in range(2):
             hidden = slice(k * HID, (k + 1) * HID)
@@ -319,9 +319,6 @@
             send_back(m, h)
 
     def home(m):
-        dispatch = dispatch_matrix(info, m)
-        combine = combine_matrix(comb_info, m)
-
         @pl.when(c == 1)
         def _():
             pl.semaphore_wait(turn, 1)
@@ -332,10 +329,14 @@
                 drain(g_prev.at[m, h], p_recv.at[m, h])
 
             arrived(recv_r, m, h, r_recv)
-            mixed = matmul(combine, recv_r[m, :, half(h), :].reshape(PAIR_ROWS, LANES))
+            mixed = matmul(combine_mat[...], recv_r[m, :, half(h), :].reshape(PAIR_ROWS, LANES))
             rows = (g_prev[m, h].astype(F32) + mixed).astype(BF16)
             g_here[m, h] = rows
-            spread_g(m, h, dispatch, rows)
+            spread_g(m, h, dispatch_mat[...], rows)
+
+    def prepare(m):
+        dispatch_mat[...] = dispatch_matrix(info, m)
+        combine_mat[...] = combine_matrix(comb_info, m)
 
     def pass_on(m):
         @pl.when(line > 0)
@@ -448,12 +449,14 @@
     @pl.when(line < LAST)
     def _():
         info_copy(0).wait_recv()
+        prepare(0)
 
     def step(n):
         @pl.when(line < LAST)
         def _():
             home(n)
             pass_on(n)
+            prepare(jnp.minimum(n + 1, MB - 1))
 
         k = n // 2
 
@@ -542,6 +545,8 @@
             pltpu.VMEM((FOLD * PAD, LANES), BF16),
             pltpu.VMEM((FOLD * PAD, PAIR_ROWS), BF16),
             pltpu.VMEM((PAIR_ROWS, FOLD * PAD), BF16),
+            pltpu.VMEM((PAIR_ROWS, TOK_ROWS), BF16),
+            pltpu.VMEM((TOK_ROWS, PAIR_ROWS), BF16),
         ]
         + [dma((3,)), dma((5,)), dma((5,)), dma((3,)), dma((3,)), dma, dma((PAIRS,))]
         + [dma] * 5

time: 450 us -> 450 us (level)
  no operation moved by 1% of the time
where the time goes in v3:
time: 450 us; the launch traced here: 445 us
  Pallas kernels  440 us (98%)
    pallas_call x1, Pallas kernels, chain(): pl.pallas_call(chain_kernel, out_shape=jax.ShapeDtypeStruct(rows, BF16),...  440 us

profile of v3, /device:TPU:32, one launch (start us, length us, event | category | flops | bytes accessed | tf_op | source)
XLA Modules:
  0.0 444.9 jit_solution(9665864164292356443)
XLA Ops:
  0.0 0.7 convert_bitcast_fusion
  0.7 0.7 bitcast_convert_fusion
  1.4 0.7 copy.10.pairs_ref
  2.2 440.4 %shard_map.73 = bf16[16,2,128,128]{3,2,1,0:T(8,128)(2,1)} custom-call(bf16[128,4096]{1,0:T(8,128)(2,1)} %bitcast.23, bf16[128,4096]{1,0:T(8,128)(2,1)} %bitcast.24, f32[4,16,128]{2,1,0:T(8,128)} %copy.10.pairs_ref, bf16[4096,256]{1,0:T(8,128)(2,1)} %bitcast.20, bf16[4096,256]{1,0:T(8,128)(2,1)} %bitcast.21, bf16[256,4096]{1,0:T(8,128)(2,1)} %bitcast.22), custom_call_target="tpu_custom_call" | custom-call | tf_op jit(solution)/shard_map/pallas_call | solution.py:527
  442.6 2.3 copy.12
  (3 shorter events, 0.0 us)
